TPU v7x, 32 devices: a whole 2x2x4 slice. The times are simulated.
32 devices in a mesh: groups: 2 (over y), sec: 4 (over z), mpo: 2 (over x), rep: 2 (over core).
Axes of the slice: x: 2, y: 2, z: 4, core: 2. Of those that a mesh axis runs over, the one named last changes fastest.
Arguments:
- wave: bfloat16 [16, 128, 16, 256], P(('groups', 'sec'), None, None, 'rep'), parts along dimension 0, may hold values from -6 to 6
- left_env: bfloat16 [16, 8, 128, 128], P(('groups', 'mpo'), 'sec'), parts along dimension 0, may hold values from -0.5 to 0.5
- right_env: bfloat16 [16, 8, 256, 256], P(('groups', 'mpo'), 'sec', 'rep'), parts along dimension 0, may hold values from -0.375 to 0.375
- phys_op: bfloat16 [16, 16, 16], P(('groups', 'mpo')), parts along dimension 0, may hold values from -0.5 to 0.5
- source: int32 [16, 8], P(('groups', 'mpo')), parts along dimension 0, may hold values from 0 to 7, each once within a row
- sector_rows: int32 [16], P('groups'), parts along dimension 0, may hold values from 64 to 128, as said below
Outputs:
- product: float32 [16, 128, 16, 256], P(('groups', 'sec'), None, 'mpo', 'rep'), parts along dimension 0
There are 2 independent parts, one for each index of `groups`. A program takes and returns all parts, laid end to end along the dimension named above; each array names one. Nothing has to cross between parts.
Inputs may be any that keep to these rules, and one draw needn't show every extreme that they name: `source`: each row is a permutation of the 8 sectors. `sector_rows`: rows of a block at or beyond its sector's count are ignored; some sector is full.
All inputs are finite; a program needn't handle non-finite values.
Results may differ from a plain program's by a relative error of at most 0.005.
Values may be sent and summed in bfloat16 or wider, within the bound.
A program may use at most 64 MiB of HBM per device.

v0:
```python
import jax
import jax.numpy as jnp
from jax import lax
from jax.sharding import PartitionSpec as P


def per_device(wave, left_env, right_env, phys_op, source, sector_rows):
    sectors = wave.shape[0]
    rows_full = wave.shape[1]
    phys_all = wave.shape[2]
    local_cols = wave.shape[3]
    terms_here = phys_op.shape[0]
    sec_count = lax.axis_size("sec")
    mpo_count = lax.axis_size("mpo")
    group_states = phys_all // mpo_count
    piece_len = rows_full * group_states * local_cols // sec_count
    position = lax.axis_index("sec")
    own_rows = lax.dynamic_slice_in_dim(sector_rows, position * sectors, sectors)
    keep = jnp.arange(rows_full, dtype=jnp.int32)[None, :] < own_rows[:, None]
    masked = jnp.where(keep[:, :, None, None], wave, jnp.zeros_like(wave))
    full_wave = lax.all_gather(masked, "rep", axis=3, tiled=True)
    phys = jnp.einsum(
        "alpr,wqp->walqr", full_wave, phys_op, preferred_element_type=jnp.float32
    ).astype(jnp.bfloat16)
    right = jnp.einsum(
        "walqr,wasr->walqs", phys, right_env, preferred_element_type=jnp.float32
    ).astype(jnp.bfloat16)
    right_grouped = right.reshape(
        terms_here, sectors, rows_full, mpo_count, group_states, local_cols
    )
    moved = jnp.einsum(
        "waml,walgks->wagmks", left_env, right_grouped, preferred_element_type=jnp.float32
    ).astype(jnp.bfloat16)
    flat_moved = moved.reshape(terms_here, sectors, mpo_count, sec_count, piece_len)
    columns = lax.all_to_all(flat_moved, "sec", split_axis=3, concat_axis=1, tiled=True)

    def pick_term(block_set, order):
        return jnp.take(block_set, order, axis=0)

    picked = jax.vmap(pick_term)(columns, source)
    summed_terms = jnp.sum(picked.astype(jnp.float32), axis=0)
    returned = lax.all_to_all(summed_terms, "sec", split_axis=0, concat_axis=2, tiled=True)
    finished = lax.psum_scatter(returned, "mpo", scatter_dimension=1, tiled=True)
    product = finished.reshape(sectors, rows_full, group_states, local_cols)
    return jnp.where(keep[:, :, None, None], product, jnp.zeros_like(product))


def solution(mesh):
    placed = (
        P(("groups", "sec"), None, None, "rep"),
        P(("groups", "mpo"), "sec", None, None),
        P(("groups", "mpo"), "sec", "rep", None),
        P(("groups", "mpo"), None, None),
        P(("groups", "mpo"), None),
        P("groups"),
    )
    return jax.shard_map(
        per_device,
        mesh=mesh,
        in_specs=placed,
        out_specs=P(("groups", "sec"), None, "mpo", "rep"),
        check_vma=False,
    )
```

profile of v0, /device:TPU:1, one launch (start us, length us, event | category | flops | bytes accessed | tf_op | source)
XLA Modules:
  0.0 317.0 jit_solution(8658140300643781514)
XLA Ops:
  6.5 0.0 copy-start
  6.5 0.0 all-gather.2.cloned.1.call-start
  6.5 0.8 dynamic_slice.3
  7.3 0.1 iota_compare_fusion
  7.4 2.3 broadcast_select_fusion
  9.7 0.0 all-gather.2.cloned.1.call-update
  9.7 13.0 %all-gather.2.cloned.1.call-done = bf16[2,128,16,256]{3,2,1,0:T(8,128)(2,1)} async-done(((bf16[2,128,16,128]{3,2,1,0:T(8,128)(2,1)}), bf16[2,128,16,256]{3,2,1,0:T(8,128)(2,1)}) %all-gather.2.cloned.1.call-update) | async-done | bytes 2097168 | tf_op jit(solution)/shard_map/all_gather | solution.py:21
  22.7 3.9 %convert_bitcast_fusion = bf16[4,2,128,16,256]{4,3,0,2,1:T(8,128)(2,1)S(1)} fusion(bf16[2,128,16,256]{3,2,1,0:T(8,128)(2,1)} %all-gather.2.cloned.1.call-done, bf16[4,16,16]{2,1,0:T(8,128)(2,1)} %param.9), kind=kOutput, calls=%fused_computation.4 | convolution fusion | flops 138412032 | bytes 10487808 | tf_op jit(solution)/shard_map/alpr,wqp->walqr/dot_general | solution.py:22
  26.6 0.0 copy-done
  26.6 0.0 copy-start.1
  26.6 9.4 %fusion.2 = bf16[4,2,128,16,128]{4,2,3,1,0:T(8,128)(2,1)S(1)} fusion(bf16[4,2,128,16,256]{4,3,0,2,1:T(8,128)(2,1)S(1)} %convert_bitcast_fusion, bf16[4,2,128,256]{3,2,1,0:T(8,128)(2,1)S(1)} %copy-done), kind=kOutput, calls=%fused_computation.7 | convolution fusion | flops 1075838976 | bytes 13107200 | tf_op jit(solution)/shard_map/walqr,wasr->walqs/dot_general | solution.py:25
  36.0 3.6 %convert_bitcast_fusion.1 = bf16[4,2,2,128,8,128]{3,5,4,2,1,0:T(8,128)(2,1)} fusion(bf16[4,2,128,2,8,128]{5,2,4,3,1,0:T(8,128)(2,1)S(1)} %bitcast.52, bf16[4,2,128,128]{3,2,1,0:T(8,128)(2,1)S(1)} %copy-done.1), kind=kOutput, calls=%fused_computation.6 | convolution fusion | flops 538968064 | bytes 8650752 | tf_op jit(solution)/shard_map/waml,walgks->wagmks/dot_general | solution.py:31
  39.6 7.4 %copy.20 = bf16[4,2,2,128,8,128]{5,4,3,2,1,0:T(8,128)(2,1)} copy(bf16[4,2,2,128,8,128]{3,5,4,2,1,0:T(8,128)(2,1)} %convert_bitcast_fusion.1) | data formatting | bytes 8388608 | tf_op jit(solution)/shard_map/convert_element_type | solution.py:33
  47.0 7.2 %reshape.49 = bf16[4,2,2,4,32768]{4,3,2,1,0:T(4,128)(2,1)} reshape(bf16[4,2,2,128,8,128]{5,4,3,2,1,0:T(8,128)(2,1)} %copy.20) | data formatting | bytes 8388608 | tf_op jit(solution)/shard_map/reshape | solution.py:34
  54.2 8.5 %copy.21 = bf16[4,2,2,4,32768]{4,2,1,0,3:T(2,128)(2,1)} copy(bf16[4,2,2,4,32768]{4,3,2,1,0:T(4,128)(2,1)} %reshape.49) | data formatting | bytes 8388608 | tf_op jit(solution)/shard_map/reshape | solution.py:34
  62.7 5.0 %all-to-all-start = ((bf16[4,2,2,4,32768]{4,2,1,0,3:T(2,128)(2,1)}), bf16[4,2,2,4,32768]{4,2,1,0,3:T(2,128)(2,1)}, u32[]{:S(2)}, u32[]{:S(2)}) async-start(bf16[4,2,2,4,32768]{4,2,1,0,3:T(2,128)(2,1)} %copy.21), calls=%async_computation | async-start | bytes 8388608 | tf_op jit(solution)/shard_map/all_to_all | solution.py:35
  67.6 0.0 all-reduce.3.cloned.1.call-start
  67.7 0.1 reshape.53
  67.8 93.1 %all-to-all-done = bf16[4,2,2,4,32768]{4,2,1,0,3:T(2,128)(2,1)} async-done(((bf16[4,2,2,4,32768]{4,2,1,0,3:T(2,128)(2,1)}), bf16[4,2,2,4,32768]{4,2,1,0,3:T(2,128)(2,1)}, u32[]{:S(2)}, u32[]{:S(2)}) %all-to-all-start) | async-done | bytes 4194336 | tf_op jit(solution)/shard_map/all_to_all | solution.py:35
  160.9 9.1 %copy.22 = bf16[4,4,2,2,1,32768]{5,3,2,1,0,4:T(2,128)(2,1)} copy(bf16[4,4,2,2,1,32768]{5,3,2,0,1,4:T(2,128)(2,1)} %bitcast.12) | data formatting | bytes 8388608 | tf_op jit(solution)/shard_map/all_to_all | solution.py:35
  170.0 12.7 %gather_fusion = bf16[32,2,32768]{2,1,0:T(2,128)(2,1)} fusion(bf16[4,8,2,32768]{3,2,1,0:T(2,128)(2,1)} %bitcast.49, s32[32]{0:T(128)S(1)} %reshape.53), kind=kCustom, calls=%fused_computation | custom fusion | bytes 8388864 | tf_op jit(solution)/shard_map/vmap(jit(_take))/gather | solution.py:38
  182.8 5.8 %convert_reduce_fusion = f32[8,2,32768]{2,0,1:T(8,128)S(1)} fusion(bf16[32,2,32768]{2,1,0:T(2,128)(2,1)} %gather_fusion, pred[4,8]{1,0:T(4,128)(4,1)S(1)} %compare_and_fusion), kind=kLoop, calls=%fused_computation.3 | loop fusion | flops 5767168 | bytes 6291488 | tf_op jit(solution)/shard_map/reduce_sum | solution.py:41
  188.6 1.6 copy.24
  190.2 49.7 %all_to_all.36 = f32[8,2,1,32768]{3,1,2,0:T(2,128)S(1)} all-to-all(f32[8,2,1,32768]{3,1,2,0:T(2,128)S(1)} %copy.24), channel_id=1, replica_groups=mesh['groups'=2,'sec'=4,'mpo'=2,'rep'=2] {'sec'}, dimensions={0} | all-to-all | bytes 4194304 | tf_op jit(solution)/shard_map/all_to_all | solution.py:42
  239.9 2.7 copy.25
  242.6 0.0 all-reduce.3.cloned.1.call-update
  242.6 0.0 copy-done.3
  242.6 0.6 dynamic-slice
  243.2 62.9 %all-reduce.3.cloned.1.call-done = f32[2,2,4,32768]{3,2,0,1:T(4,128)} async-done(((f32[2,2,4,32768]{3,2,0,1:T(4,128)}), f32[2,2,4,32768]{3,2,0,1:T(4,128)}) %all-reduce.3.cloned.1.call-update) | async-done | bytes 2097168
  306.1 1.9 constant_dynamic-slice_fusion
  308.1 0.7 reshape.50
  308.8 1.3 broadcast_select_fusion.1
  (6 shorter events, 0.0 us)
Async XLA Ops:
  6.5 20.0 %copy-start = (bf16[4,2,128,256]{3,2,1,0:T(8,128)(2,1)S(1)}, bf16[4,2,128,256]{3,2,1,0:T(8,128)(2,1)}, u32[]{:S(2)}) copy-start(bf16[4,2,128,256]{3,2,1,0:T(8,128)(2,1)} %param.8) | copy-start | bytes 1572868
  6.5 16.1 %all-gather.2.cloned.1.call-start = ((), (), s32[]{:S(2)}) async-start(), calls=%async_computation.2 | async-start | bytes 3145728 | tf_op jit(solution)/shard_map/all_gather | solution.py:21
  26.6 9.4 %copy-start.1 = (bf16[4,2,128,128]{3,2,1,0:T(8,128)(2,1)S(1)}, bf16[4,2,128,128]{3,2,1,0:T(8,128)(2,1)}, u32[]{:S(2)}) copy-start(bf16[4,2,128,128]{3,2,1,0:T(8,128)(2,1)} %param.7) | copy-start | bytes 786436
  62.7 5.0 %copy-start.2 = (s32[4,8]{1,0:T(4,128)S(1)}, s32[4,8]{1,0:T(4,128)}, u32[]{:S(2)}) copy-start(s32[4,8]{1,0:T(4,128)} %param.10) | copy-start | bytes 388
  62.7 98.2 %all-to-all-start = ((bf16[4,2,2,4,32768]{4,2,1,0,3:T(2,128)(2,1)}), bf16[4,2,2,4,32768]{4,2,1,0,3:T(2,128)(2,1)}, u32[]{:S(2)}, u32[]{:S(2)}) async-start(bf16[4,2,2,4,32768]{4,2,1,0,3:T(2,128)(2,1)} %copy.21), calls=%async_computation | async-start | bytes 8388608 | tf_op jit(solution)/shard_map/all_to_all | solution.py:35
  67.6 238.5 %all-reduce.3.cloned.1.call-start = ((), (), s32[]{:S(2)}) async-start(), calls=%async_computation.3 | async-start | bytes 4194304
  239.9 2.7 copy-start.3
Sparse Core Ops, SparseCore 0:
  9.8 12.7 all-gather.1
  242.7 63.3 all-reduce.2
where the time goes:
time: 318 us; the launch traced here: 317 us
  waiting for transfers between devices  169 us (53%)
  local copies, waits for them, and re-layouts  53.4 us (17%)
  blocking collectives  49.7 us (16%)
  matrix products  16.9 us (5%)
  between operations  13.5 us (4%)
  other arithmetic  9.48 us (3%)
  starting transfers between devices  5.01 us (2%)
    all_to_all x1, waiting for transfers between devices, per_device(): lax.all_to_all(flat_moved, 'sec', split_axis=3, concat_axis=1, tiled=True)  93.1 us
    unnamed x3, waiting for transfers between devices  63 us
    all_to_all x1, blocking collectives, per_device(): lax.all_to_all(summed_terms, 'sec', split_axis=0, concat_axis=2, tiled=True)  49.7 us
    reshape x2, local copies, waits for them, and re-layouts, per_device(): moved.reshape(terms_here, sectors, mpo_count, sec_count, piece_len)  15.7 us
    all_gather x1, waiting for transfers between devices, per_device(): full_wave = lax.all_gather(masked, 'rep', axis=3, tiled=True)  13 us
    gather x2, local copies, waits for them, and re-layouts, pick_term(): return jnp.take(block_set, order, axis=0)  12.8 us
    dot_general x1, matrix products, per_device(): jnp.einsum('walqr,wasr->walqs', phys, right_env, preferred_element_type=j...  9.39 us
    all_to_all x1, local copies, waits for them, and re-layouts, per_device(): lax.all_to_all(flat_moved, 'sec', split_axis=3, concat_axis=1, tiled=True)  9.15 us
  transfers between devices with their start and end apart: 3, of which 3 were waited for; matrix products, arithmetic and copies ran while one was open for 0% of the time, Pallas kernels for 0%

commit v1 on v0

v1 whole, which is shorter than its diff:
```python
import functools

import jax
import jax.numpy as jnp
from jax import lax
from jax.experimental import pallas as pl
from jax.experimental.pallas import tpu as pltpu
from jax.sharding import PartitionSpec as P

MESH = pl.DeviceIdType.MESH
GROUP = 16


def signal(sem, where):
    pl.semaphore_signal(sem, inc=1, device_id=where, device_id_type=MESH)


def kernel(
    sec_count, mpo_count, q_here,
    source_ref, rows_ref, wave_ref, left_ref, right_ref, op_ref,
    out_ref,
    wbuf, lbuf, rbuf, ph, rt, acc, sendbuf, from_left, from_right,
    wave_sems, left_sems, right_sems, send_sems, fl_sems, fr_sems, local_sems,
):
    sec = lax.axis_index("sec")
    mpo = lax.axis_index("mpo")
    rep = lax.axis_index("rep")
    sectors, dl = left_ref.shape[1], left_ref.shape[2]
    local_terms = left_ref.shape[0]
    terms = local_terms * mpo_count
    cols = right_ref.shape[2]
    depth = wbuf.shape[2] // dl

    barrier = pltpu.get_barrier_semaphore()
    signal(barrier, {"rep": 1 - rep})
    for step in range(1, mpo_count):
        signal(barrier, {"mpo": lax.rem(mpo + step, mpo_count)})

    @pl.when(sec > 0)
    def _():
        signal(barrier, {"sec": sec - 1})

    @pl.when(sec < sec_count - 1)
    def _():
        signal(barrier, {"sec": sec + 1})

    neighbours = (sec > 0).astype(jnp.int32) + (sec < sec_count - 1).astype(jnp.int32)
    pl.semaphore_wait(barrier, mpo_count + neighbours)

    wave_copy = pltpu.make_async_remote_copy(
        src_ref=wave_ref, dst_ref=wbuf.at[rep],
        send_sem=wave_sems.at[0], recv_sem=wave_sems.at[1],
        device_id={"rep": 1 - rep}, device_id_type=MESH,
    )
    wave_copy.start()
    env_copies = []
    for step in range(1, mpo_count):
        peer = {"mpo": lax.rem(mpo + step, mpo_count)}
        for ref, buf, sems in ((left_ref, lbuf, left_sems), (right_ref, rbuf, right_sems)):
            copy = pltpu.make_async_remote_copy(
                src_ref=ref, dst_ref=buf.at[mpo],
                send_sem=sems.at[0, step], recv_sem=sems.at[1, step],
                device_id=peer, device_id_type=MESH,
            )
            copy.start()
            env_copies.append(copy)
    own_wave = pltpu.make_async_copy(wave_ref, wbuf.at[rep], local_sems.at[0])
    own_left = pltpu.make_async_copy(left_ref, lbuf.at[mpo], local_sems.at[1])
    own_right = pltpu.make_async_copy(right_ref, rbuf.at[mpo], local_sems.at[2])
    own_wave.start()
    own_left.start()
    own_right.start()
    own_wave.wait()
    wave_copy.wait()

    def transform(part, group):
        rows = pl.ds(pl.multiple_of(group * (GROUP * depth), GROUP * depth), GROUP * depth)
        both = jnp.concatenate([wbuf[0, part, rows, :], wbuf[1, part, rows, :]], axis=1)
        result = jnp.dot(op_ref[...], both, preferred_element_type=jnp.float32)
        l_rows = pl.ds(pl.multiple_of(group * GROUP, GROUP), GROUP)
        ph[part, :, l_rows, :] = result.astype(jnp.bfloat16).reshape(
            terms * q_here, GROUP, 2 * cols
        )

    for part in range(sectors):
        @pl.loop(0, dl // GROUP)
        def _(group):
            transform(part, group)

    row_index = lax.broadcasted_iota(jnp.int32, (dl, cols), 0)

    def contract(owner):
        for part in range(sectors):
            live = row_index < rows_ref[sec * sectors + part]

            @pl.loop(0, local_terms)
            def _(term):
                whole_term = owner * local_terms + term
                states = ph[part, pl.ds(whole_term * q_here, q_here)]
                result = lax.dot_general(
                    states.reshape(q_here * dl, 2 * cols),
                    rbuf[owner, term, part],
                    (((1,), (1,)), ((), ())),
                    preferred_element_type=jnp.float32,
                )
                for q in range(q_here):
                    piece = jnp.where(live, result[q * dl:(q + 1) * dl], 0.0)
                    rt[whole_term, part, :, q * cols:(q + 1) * cols] = piece.astype(jnp.bfloat16)

    own_right.wait()
    contract(mpo)
    for copy in env_copies:
        copy.wait()
    own_left.wait()
    for step in range(1, mpo_count):
        contract(lax.rem(mpo + step, mpo_count))

    width = q_here * cols
    tile = 256

    def partial(target):
        lefts, places = [], []
        for term in range(terms):
            src = source_ref[term, target] - sec * sectors
            inside = jnp.logical_and(src >= 0, src < sectors)
            place = jnp.clip(src, 0, sectors - 1)
            gate = jnp.where(inside, 1.0, 0.0)
            block = lbuf[term // local_terms, term % local_terms, place]
            lefts.append((block.astype(jnp.float32) * gate).astype(jnp.bfloat16))
            places.append(place)
        lhs = jnp.concatenate(lefts, axis=1)
        for n in range(0, width, tile):
            rhs = jnp.concatenate(
                [rt[term, places[term], :, n:n + tile] for term in range(terms)], axis=0
            )
            acc[:, n:n + tile] = jnp.dot(lhs, rhs, preferred_element_type=jnp.float32)

    def hop(owner, part, landing, sems, to):
        return pltpu.make_async_remote_copy(
            src_ref=sendbuf.at[owner, part], dst_ref=landing.at[owner, part],
            send_sem=send_sems.at[owner, part], recv_sem=sems.at[owner, part],
            device_id={"sec": to}, device_id_type=MESH,
        )

    def pass_on(owner, part, inner, landing, sems, to):
        partial(owner * sectors + part)

        @pl.when(inner)
        def _():
            hop(owner, part, landing, sems, to).wait_recv()
            acc[...] += landing[owner, part].astype(jnp.float32)

        sendbuf[owner, part] = acc[...].astype(jnp.bfloat16)
        hop(owner, part, landing, sems, to).start()

    up = lax.rem(sec + 1, sec_count)
    down = lax.rem(sec + sec_count - 1, sec_count)

    @pl.loop(0, sec_count - 1)
    def _(step):
        above = sec + sec_count - 1 - step
        below = step - (sec_count - 1) + sec

        @pl.when(above < sec_count)
        def _():
            @pl.loop(0, sectors)
            def _(part):
                pass_on(above, part, sec > 0, from_left, fl_sems, up)

        @pl.when(below >= 0)
        def _():
            @pl.loop(0, sectors)
            def _(part):
                pass_on(below, part, sec < sec_count - 1, from_right, fr_sems, down)

    for part in range(sectors):
        partial(sec * sectors + part)

        @pl.when(sec > 0)
        def _():
            hop(sec, part, from_left, fl_sems, up).wait_recv()
            acc[...] += from_left[sec, part].astype(jnp.float32)

        @pl.when(sec < sec_count - 1)
        def _():
            hop(sec, part, from_right, fr_sems, down).wait_recv()
            acc[...] += from_right[sec, part].astype(jnp.float32)

        live = row_index < rows_ref[sec * sectors + part]
        for q in range(q_here):
            columns = slice(q * cols, (q + 1) * cols)
            out_ref[part, :, columns] = jnp.where(live, acc[:, columns], 0.0)

    @pl.loop(0, sec_count)
    def _(owner):
        @pl.when(owner != sec)
        def _():
            for part in range(sectors):
                hop(owner, part, from_left, fl_sems, up).wait_send()


def per_device(sec_count, mpo_count, wave, left_env, right_env, phys_op, source, sector_rows):
    sectors, dl, phys_all, cols = wave.shape
    local_terms = phys_op.shape[0]
    terms = local_terms * mpo_count
    q_here = phys_all // mpo_count
    mpo = lax.axis_index("mpo")
    small = jnp.concatenate(
        [phys_op.reshape(local_terms, -1), source.astype(jnp.bfloat16)], axis=1
    )
    small = lax.all_gather(small, "mpo", axis=0, tiled=True)
    ops = small[:, :phys_all * phys_all].reshape(terms, phys_all, phys_all)
    order = small[:, phys_all * phys_all:].astype(jnp.int32)
    ops = lax.dynamic_slice_in_dim(ops, mpo * q_here, q_here, axis=1)
    same = jnp.eye(GROUP, dtype=jnp.bfloat16)
    spread = (ops[:, :, None, None, :] * same[None, None, :, :, None]).reshape(
        terms * q_here * GROUP, GROUP * phys_all
    )
    vmem = pl.BlockSpec(memory_space=pltpu.VMEM)
    smem = pl.BlockSpec(memory_space=pltpu.SMEM)
    width = q_here * cols
    bf16 = jnp.bfloat16
    out = pl.pallas_call(
        functools.partial(kernel, sec_count, mpo_count, q_here),
        out_shape=jax.ShapeDtypeStruct((sectors, dl, width), jnp.float32),
        in_specs=[smem, smem, vmem, vmem, vmem, vmem],
        out_specs=vmem,
        scratch_shapes=[
            pltpu.VMEM((2, sectors, dl * phys_all, cols), bf16),
            pltpu.VMEM((mpo_count,) + left_env.shape, bf16),
            pltpu.VMEM((mpo_count,) + right_env.shape, bf16),
            pltpu.VMEM((sectors, terms * q_here, dl, 2 * cols), bf16),
            pltpu.VMEM((terms, sectors, dl, width), bf16),
            pltpu.VMEM((dl, width), jnp.float32),
            pltpu.VMEM((sec_count, sectors, dl, width), bf16),
            pltpu.VMEM((sec_count, sectors, dl, width), bf16),
            pltpu.VMEM((sec_count, sectors, dl, width), bf16),
            pltpu.SemaphoreType.DMA((2,)),
            pltpu.SemaphoreType.DMA((2, mpo_count)),
            pltpu.SemaphoreType.DMA((2, mpo_count)),
            pltpu.SemaphoreType.DMA((sec_count, sectors)),
            pltpu.SemaphoreType.DMA((sec_count, sectors)),
            pltpu.SemaphoreType.DMA((sec_count, sectors)),
            pltpu.SemaphoreType.DMA((3,)),
        ],
        compiler_params=pltpu.CompilerParams(
            collective_id=0, has_side_effects=True, vmem_limit_bytes=56 * 1024 * 1024
        ),
        cost_estimate=pl.CostEstimate(
            flops=6 * 10**9, bytes_accessed=8 * 2**20, transcendentals=0
        ),
    )(
        order, sector_rows, wave.reshape(sectors, dl * phys_all, cols),
        left_env, right_env, spread,
    )
    return out.reshape(sectors, dl, q_here, cols)


def solution(mesh):
    placed = (
        P(("groups", "sec"), None, None, "rep"),
        P(("groups", "mpo"), "sec", None, None),
        P(("groups", "mpo"), "sec", "rep", None),
        P(("groups", "mpo"), None, None),
        P(("groups", "mpo"), None),
        P("groups"),
    )
    return jax.shard_map(
        functools.partial(per_device, mesh.shape["sec"], mesh.shape["mpo"]),
        mesh=mesh,
        in_specs=placed,
        out_specs=P(("groups", "sec"), None, "mpo", "rep"),
        check_vma=False,
    )
```

time: 318 us -> 79.1 us (0.25)
  the two profiles are of different devices: /device:TPU:1 before, /device:TPU:20 now
where the time goes in v1:
time: 79.1 us; the launch traced here: 78.8 us
  Pallas kernels  61.3 us (77%)
  local copies, waits for them, and re-layouts  9.55 us (12%)
  blocking collectives  4.33 us (5%)
  other arithmetic  3.59 us (5%)
    pallas_call x1, Pallas kernels, per_device(): pl.pallas_call(functools.partial(kernel, sec_count, mpo_count, q_here), o...  61.3 us
    mul x1, local copies, waits for them, and re-layouts, per_device(): ops[:, :, None, None, :] * same[None, None, :, :, None]  6.23 us
    all_gather x1, blocking collectives, per_device(): small = lax.all_gather(small, 'mpo', axis=0, tiled=True)  4.33 us
    unnamed x2, local copies, waits for them, and re-layouts  2.41 us
    mul x1, other arithmetic, per_device(): ops[:, :, None, None, :] * same[None, None, :, :, None]  2.29 us

profile of v1, /device:TPU:20, one launch (start us, length us, event | category | flops | bytes accessed | tf_op | source)
XLA Modules:
  0.0 78.8 jit_solution(473063222273213708)
XLA Ops:
  0.0 0.7 convert_element_type.13
  0.7 0.8 %reshape.25 = bf16[4,256]{1,0:T(4,128)(2,1)S(1)} reshape(bf16[4,16,16]{2,1,0:T(8,128)(2,1)} %param.9) | data formatting | bytes 4096 | tf_op jit(solution)/shard_map/reshape | solution.py:209
  1.5 4.3 %all-gather = bf16[2,4,264]{2,1,0:T(4,128)(2,1)S(1)} all-gather(bf16[1,4,264]{2,1,0:T(4,128)(2,1)S(1)} %maximum_bitcast_fusion), channel_id=1, replica_groups=mesh['groups'=2,'sec'=4,'mpo'=2,'rep'=2] {'mpo'}, dimensions={0}, use_global_device_ids=true | all-gather | bytes 6336 | tf_op jit(solution)/shard_map/all_gather | solution.py:211
  5.9 0.6 slice_convert_fusion.source_ref
  6.5 0.1 reshape.27
  6.6 2.3 %broadcast_multiply_fusion = bf16[8,8,16,16,16]{4,3,2,1,0:T(8,128)(2,1)} fusion(bf16[16,16]{1,0:T(8,128)(2,1)S(1)} %fusion, bf16[8,8,16]{2,1,0:T(8,128)(2,1)S(1)} %constant_dynamic-slice_fusion), kind=kLoop, calls=%fused_computation | loop fusion | flops 262144 | bytes 526848 | tf_op jit(solution)/shard_map/mul | solution.py:216
  8.9 6.2 %mul.24.op_ref = bf16[1024,256]{1,0:T(8,128)(2,1)} reshape(bf16[8,8,16,16,16]{4,3,2,1,0:T(8,128)(2,1)} %broadcast_multiply_fusion) | data formatting | bytes 1048576 | tf_op jit(solution)/shard_map/mul | solution.py:216
  15.1 61.3 %shard_map.64 = f32[2,128,1024]{2,1,0:T(8,128)} custom-call(s32[8,8]{1,0:T(8,128)} %slice_convert_fusion.source_ref, s32[8]{0:T(128)} %rows_ref.1, bf16[2,2048,128]{2,1,0:T(8,128)(2,1)} %bitcast.10, bf16[4,2,128,128]{3,2,1,0:T(8,128)(2,1)} %left_ref.1, bf16[4,2,128,256]{3,2,1,0:T(8,128)(2,1)} %right_ref.1, bf16[1024,256]{1,0:T(8,128)(2,1)} %mul.24.op_ref), custom_call_target="tpu_custom_call" | custom-call | flops 6000000000 | bytes 8388608 | tf_op jit(solution)/shard_map/pallas_call | solution.py:223
  76.4 2.4 %copy.7 = f32[32,8,8,128]{3,2,1,0:T(8,128)} copy(f32[32,8,8,128]{3,1,2,0:T(8,128)} %bitcast.9) | data formatting | bytes 2097152
  (5 shorter events, 0.0 us)

commit v2 on v1

--- a/solution.py
+++ b/solution.py
@@ -17,10 +17,10 @@
 
 def kernel(
     sec_count, mpo_count, q_here,
-    source_ref, rows_ref, wave_ref, left_ref, right_ref, op_ref,
+    source_ref, rows_ref, wave_ref, left_ref, right_ref, phys_ref,
     out_ref,
-    wbuf, lbuf, rbuf, ph, rt, acc, sendbuf, from_left, from_right,
-    wave_sems, left_sems, right_sems, send_sems, fl_sems, fr_sems, local_sems,
+    order_buf, order, pbuf, op_ref, wbuf, lbuf, rbuf, ph, rt, acc, sendbuf, from_left, from_right,
+    wave_sems, small_sems, left_sems, right_sems, send_sems, fl_sems, fr_sems, local_sems, turn,
 ):
     sec = lax.axis_index("sec")
     mpo = lax.axis_index("mpo")
@@ -52,24 +52,58 @@
         send_sem=wave_sems.at[0], recv_sem=wave_sems.at[1],
         device_id={"rep": 1 - rep}, device_id_type=MESH,
     )
-    wave_copy.start()
-    env_copies = []
-    for step in range(1, mpo_count):
-        peer = {"mpo": lax.rem(mpo + step, mpo_count)}
-        for ref, buf, sems in ((left_ref, lbuf, left_sems), (right_ref, rbuf, right_sems)):
-            copy = pltpu.make_async_remote_copy(
+
+    def to_peers(ref, buf, sems):
+        return [
+            pltpu.make_async_remote_copy(
                 src_ref=ref, dst_ref=buf.at[mpo],
                 send_sem=sems.at[0, step], recv_sem=sems.at[1, step],
-                device_id=peer, device_id_type=MESH,
+                device_id={"mpo": lax.rem(mpo + step, mpo_count)}, device_id_type=MESH,
             )
+            for step in range(1, mpo_count)
+        ]
+
+    phys_copies = to_peers(phys_ref, pbuf, small_sems.at[0])
+    order_copies = to_peers(source_ref, order_buf, small_sems.at[1])
+    right_copies = to_peers(right_ref, rbuf, right_sems)
+    left_copies = to_peers(left_ref, lbuf, left_sems)
+    env_copies = right_copies + left_copies
+    for copy in phys_copies + order_copies:
+        copy.start()
+    wave_copy.start()
+
+    @pl.when(rep == 0)
+    def _():
+        for copy in env_copies:
             copy.start()
-            env_copies.append(copy)
+
     own_wave = pltpu.make_async_copy(wave_ref, wbuf.at[rep], local_sems.at[0])
     own_left = pltpu.make_async_copy(left_ref, lbuf.at[mpo], local_sems.at[1])
     own_right = pltpu.make_async_copy(right_ref, rbuf.at[mpo], local_sems.at[2])
     own_wave.start()
     own_left.start()
     own_right.start()
+    pbuf[mpo] = phys_ref[...]
+    order_buf[mpo] = source_ref[...]
+    for copy in phys_copies + order_copies:
+        copy.wait()
+    to_scalars = pltpu.make_async_copy(order_buf, order, local_sems.at[3])
+    to_scalars.start()
+    phys_all = phys_ref.shape[1]
+    spread_rows, spread_cols = op_ref.shape
+    flat = pbuf[...].reshape(terms * phys_all, phys_all)
+    r = lax.broadcasted_iota(jnp.int32, (spread_rows, terms * phys_all), 0) // GROUP
+    c = lax.broadcasted_iota(jnp.int32, (spread_rows, terms * phys_all), 1)
+    want = (r // q_here) * phys_all + mpo * q_here + r % q_here
+    pick = jnp.where(want == c, 1.0, 0.0).astype(jnp.bfloat16)
+    tall = jnp.dot(pick, flat, preferred_element_type=jnp.float32).astype(jnp.bfloat16)
+    p = lax.broadcasted_iota(jnp.int32, (phys_all, spread_cols), 0)
+    c = lax.broadcasted_iota(jnp.int32, (phys_all, spread_cols), 1)
+    repeat = jnp.where(c % phys_all == p, 1.0, 0.0).astype(jnp.bfloat16)
+    wide = jnp.dot(tall, repeat, preferred_element_type=jnp.float32)
+    r = lax.broadcasted_iota(jnp.int32, (spread_rows, spread_cols), 0)
+    c = lax.broadcasted_iota(jnp.int32, (spread_rows, spread_cols), 1)
+    op_ref[...] = jnp.where(r % GROUP == c // phys_all, wide, 0.0).astype(jnp.bfloat16)
     own_wave.wait()
     wave_copy.wait()
 
@@ -109,11 +143,26 @@
 
     own_right.wait()
     contract(mpo)
-    for copy in env_copies:
-        copy.wait()
+
+    @pl.when(rep == 0)
+    def _():
+        for copy in env_copies:
+            copy.wait_send()
+        signal(turn, {"rep": 1})
+
+    @pl.when(rep == 1)
+    def _():
+        pl.semaphore_wait(turn, 1)
+        for copy in env_copies:
+            copy.start()
+
+    for step in range(1, mpo_count):
+        right_copies[step - 1].wait_recv()
+        contract(lax.rem(mpo + mpo_count - step, mpo_count))
     own_left.wait()
-    for step in range(1, mpo_count):
-        contract(lax.rem(mpo + step, mpo_count))
+    to_scalars.wait()
+    for copy in left_copies:
+        copy.wait_recv()
 
     width = q_here * cols
     tile = 256
@@ -121,7 +170,7 @@
     def partial(target):
         lefts, places = [], []
         for term in range(terms):
-            src = source_ref[term, target] - sec * sectors
+            src = order[term // local_terms, term % local_terms, target] - sec * sectors
             inside = jnp.logical_and(src >= 0, src < sectors)
             place = jnp.clip(src, 0, sectors - 1)
             gate = jnp.where(inside, 1.0, 0.0)
@@ -198,24 +247,17 @@
             for part in range(sectors):
                 hop(owner, part, from_left, fl_sems, up).wait_send()
 
+    @pl.when(rep == 1)
+    def _():
+        for copy in env_copies:
+            copy.wait_send()
+
 
 def per_device(sec_count, mpo_count, wave, left_env, right_env, phys_op, source, sector_rows):
     sectors, dl, phys_all, cols = wave.shape
     local_terms = phys_op.shape[0]
     terms = local_terms * mpo_count
     q_here = phys_all // mpo_count
-    mpo = lax.axis_index("mpo")
-    small = jnp.concatenate(
-        [phys_op.reshape(local_terms, -1), source.astype(jnp.bfloat16)], axis=1
-    )
-    small = lax.all_gather(small, "mpo", axis=0, tiled=True)
-    ops = small[:, :phys_all * phys_all].reshape(terms, phys_all, phys_all)
-    order = small[:, phys_all * phys_all:].astype(jnp.int32)
-    ops = lax.dynamic_slice_in_dim(ops, mpo * q_here, q_here, axis=1)
-    same = jnp.eye(GROUP, dtype=jnp.bfloat16)
-    spread = (ops[:, :, None, None, :] * same[None, None, :, :, None]).reshape(
-        terms * q_here * GROUP, GROUP * phys_all
-    )
     vmem = pl.BlockSpec(memory_space=pltpu.VMEM)
     smem = pl.BlockSpec(memory_space=pltpu.SMEM)
     width = q_here * cols
@@ -223,9 +265,13 @@
     out = pl.pallas_call(
         functools.partial(kernel, sec_count, mpo_count, q_here),
         out_shape=jax.ShapeDtypeStruct((sectors, dl, width), jnp.float32),
-        in_specs=[smem, smem, vmem, vmem, vmem, vmem],
+        in_specs=[vmem, smem, vmem, vmem, vmem, vmem],
         out_specs=vmem,
         scratch_shapes=[
+            pltpu.VMEM((mpo_count,) + source.shape, jnp.int32),
+            pltpu.SMEM((mpo_count,) + source.shape, jnp.int32),
+            pltpu.VMEM((mpo_count,) + phys_op.shape, bf16),
+            pltpu.VMEM((terms * q_here * GROUP, GROUP * phys_all), bf16),
             pltpu.VMEM((2, sectors, dl * phys_all, cols), bf16),
             pltpu.VMEM((mpo_count,) + left_env.shape, bf16),
             pltpu.VMEM((mpo_count,) + right_env.shape, bf16),
@@ -236,12 +282,14 @@
             pltpu.VMEM((sec_count, sectors, dl, width), bf16),
             pltpu.VMEM((sec_count, sectors, dl, width), bf16),
             pltpu.SemaphoreType.DMA((2,)),
+            pltpu.SemaphoreType.DMA((2, 2, mpo_count)),
             pltpu.SemaphoreType.DMA((2, mpo_count)),
             pltpu.SemaphoreType.DMA((2, mpo_count)),
             pltpu.SemaphoreType.DMA((sec_count, sectors)),
             pltpu.SemaphoreType.DMA((sec_count, sectors)),
             pltpu.SemaphoreType.DMA((sec_count, sectors)),
-            pltpu.SemaphoreType.DMA((3,)),
+            pltpu.SemaphoreType.DMA((4,)),
+            pltpu.SemaphoreType.REGULAR,
         ],
         compiler_params=pltpu.CompilerParams(
             collective_id=0, has_side_effects=True, vmem_limit_bytes=56 * 1024 * 1024
@@ -250,8 +298,8 @@
             flops=6 * 10**9, bytes_accessed=8 * 2**20, transcendentals=0
         ),
     )(
-        order, sector_rows, wave.reshape(sectors, dl * phys_all, cols),
-        left_env, right_env, spread,
+        source, sector_rows, wave.reshape(sectors, dl * phys_all, cols),
+        left_env, right_env, phys_op,
     )
     return out.reshape(sectors, dl, q_here, cols)
 

time: 79.1 us -> 60.3 us (0.76)
  the two profiles are of different devices: /device:TPU:20 before, /device:TPU:1 now
where the time goes in v2:
time: 60.3 us; the launch traced here: 60.2 us
  Pallas kernels  57.8 us (96%)
  local copies, waits for them, and re-layouts  2.39 us (4%)
    pallas_call x1, Pallas kernels, per_device(): pl.pallas_call(functools.partial(kernel, sec_count, mpo_count, q_here), o...  57.8 us
    unnamed x1, local copies, waits for them, and re-layouts  2.39 us

profile of v2, /device:TPU:1, one launch (start us, length us, event | category | flops | bytes accessed | tf_op | source)
XLA Modules:
  0.0 60.2 jit_solution(17561599989779676781)
XLA Ops:
  0.0 57.8 %shard_map.64 = f32[2,128,1024]{2,1,0:T(8,128)} custom-call(s32[4,8]{1,0:T(4,128)} %source_ref.1, s32[8]{0:T(128)} %rows_ref.1, bf16[2,2048,128]{2,1,0:T(8,128)(2,1)} %bitcast.6, bf16[4,2,128,128]{3,2,1,0:T(8,128)(2,1)} %left_ref.1, bf16[4,2,128,256]{3,2,1,0:T(8,128)(2,1)} %right_ref.1, bf16[4,16,16]{2,1,0:T(8,128)(2,1)} %phys_ref.1), custom_call_target="tpu_custom_call" | custom-call | flops 6000000000 | bytes 8388608 | tf_op jit(solution)/shard_map/pallas_call | solution.py:265
  57.8 2.4 %copy.7 = f32[32,8,8,128]{3,2,1,0:T(8,128)} copy(f32[32,8,8,128]{3,1,2,0:T(8,128)} %bitcast.5) | data formatting | bytes 2097152

commit v3 on v2

v3 whole, which is shorter than its diff:
```python
import functools

import jax
import jax.numpy as jnp
from jax import lax
from jax.experimental import pallas as pl
from jax.experimental.pallas import tpu as pltpu
from jax.sharding import PartitionSpec as P

MESH = pl.DeviceIdType.MESH
GROUP = 16


def split(value, size):
    if size & (size - 1):
        return value // size, value % size
    return lax.shift_right_logical(value, size.bit_length() - 1), value & (size - 1)


def signal(sem, where):
    pl.semaphore_signal(sem, inc=1, device_id=where, device_id_type=MESH)


def kernel(
    sec_count, mpo_count, q_here,
    source_ref, rows_ref, wave_ref, left_ref, right_ref, phys_ref,
    out_ref,
    order_buf, order, pbuf, pick_ref, op_ref, wbuf, lbuf, rbuf, ph, rt, acc, sendbuf, from_left, from_right,
    wave_sems, small_sems, left_sems, right_sems, send_sems, fl_sems, fr_sems, local_sems, turn,
):
    sec = lax.axis_index("sec")
    mpo = lax.axis_index("mpo")
    rep = lax.axis_index("rep")
    sectors, dl = left_ref.shape[1], left_ref.shape[2]
    local_terms = left_ref.shape[0]
    terms = local_terms * mpo_count
    cols = right_ref.shape[2]
    depth = wbuf.shape[2] // dl
    chunks = rt.shape[0]
    q_chunk = q_here // chunks
    width = q_chunk * cols

    barrier = pltpu.get_barrier_semaphore()
    signal(barrier, {"rep": 1 - rep})
    for step in range(1, mpo_count):
        signal(barrier, {"mpo": lax.rem(mpo + step, mpo_count)})

    @pl.when(sec > 0)
    def _():
        signal(barrier, {"sec": sec - 1})

    @pl.when(sec < sec_count - 1)
    def _():
        signal(barrier, {"sec": sec + 1})

    phys_all = phys_ref.shape[1]
    spread_rows = op_ref.shape[0] * op_ref.shape[1]
    spread_cols = op_ref.shape[2]
    r = lax.broadcasted_iota(jnp.int32, (spread_rows, 1), 0)
    c = lax.broadcasted_iota(jnp.int32, (1, terms * phys_all), 1)
    r, lane = split(r, GROUP)
    r, q_in = split(r, q_chunk)
    chunk_of, term_of = split(r, terms)
    want = term_of * phys_all + mpo * q_here + chunk_of * q_chunk + q_in
    pick_ref[...] = jnp.where(want == c, 1.0, 0.0).astype(jnp.bfloat16)
    c = lax.broadcasted_iota(jnp.int32, (1, spread_cols), 1)
    mask = jnp.where(lane == split(c, phys_all)[0], 1.0, 0.0).astype(jnp.bfloat16)
    op_ref[...] = mask.reshape(op_ref.shape)
    neighbours = (sec > 0).astype(jnp.int32) + (sec < sec_count - 1).astype(jnp.int32)
    pl.semaphore_wait(barrier, mpo_count + neighbours)

    wave_copies = [
        pltpu.make_async_remote_copy(
            src_ref=wave_ref.at[part], dst_ref=wbuf.at[rep, part],
            send_sem=wave_sems.at[0, part], recv_sem=wave_sems.at[1, part],
            device_id={"rep": 1 - rep}, device_id_type=MESH,
        )
        for part in range(sectors)
    ]

    def to_peers(ref, buf, sems):
        return [
            pltpu.make_async_remote_copy(
                src_ref=ref, dst_ref=buf.at[mpo],
                send_sem=sems.at[0, step], recv_sem=sems.at[1, step],
                device_id={"mpo": lax.rem(mpo + step, mpo_count)}, device_id_type=MESH,
            )
            for step in range(1, mpo_count)
        ]

    phys_copies = to_peers(phys_ref, pbuf, small_sems.at[0])
    order_copies = to_peers(source_ref, order_buf, small_sems.at[1])
    right_copies = to_peers(right_ref, rbuf, right_sems)
    left_copies = to_peers(left_ref, lbuf, left_sems)
    env_copies = right_copies + left_copies
    for copy in phys_copies + order_copies:
        copy.start()
    for copy in wave_copies:
        copy.start()

    @pl.when(rep == 0)
    def _():
        for copy in env_copies:
            copy.start()

    own_wave = pltpu.make_async_copy(wave_ref, wbuf.at[rep], local_sems.at[0])
    own_left = pltpu.make_async_copy(left_ref, lbuf.at[mpo], local_sems.at[1])
    own_right = pltpu.make_async_copy(right_ref, rbuf.at[mpo], local_sems.at[2])
    own_wave.start()
    own_left.start()
    own_right.start()
    pbuf[mpo] = phys_ref[...]
    order_buf[mpo] = source_ref[...]
    for copy in phys_copies + order_copies:
        copy.wait()
    to_scalars = pltpu.make_async_copy(order_buf, order, local_sems.at[3])
    to_scalars.start()
    flat = pbuf[...].reshape(terms * phys_all, phys_all)
    tall = jnp.dot(pick_ref[...], flat, preferred_element_type=jnp.float32).astype(jnp.bfloat16)
    p = lax.broadcasted_iota(jnp.int32, (phys_all, spread_cols), 0)
    c = lax.broadcasted_iota(jnp.int32, (phys_all, spread_cols), 1)
    repeat = jnp.where(split(c, phys_all)[1] == p, 1.0, 0.0).astype(jnp.bfloat16)
    wide = jnp.dot(tall, repeat, preferred_element_type=jnp.float32).reshape(op_ref.shape)
    op_ref[...] = jnp.where(op_ref[...].astype(jnp.float32) > 0.5, wide, 0.0).astype(jnp.bfloat16)
    own_wave.wait()

    def transform(chunk, part):
        @pl.loop(0, dl // GROUP, unroll=2)
        def _(group):
            rows = pl.ds(pl.multiple_of(group * (GROUP * depth), GROUP * depth), GROUP * depth)
            both = jnp.concatenate([wbuf[0, part, rows, :], wbuf[1, part, rows, :]], axis=1)
            result = jnp.dot(op_ref[chunk], both, preferred_element_type=jnp.float32)
            l_rows = pl.ds(pl.multiple_of(group * GROUP, GROUP), GROUP)
            ph[part, :, l_rows, :] = result.astype(jnp.bfloat16).reshape(
                terms * q_chunk, GROUP, 2 * cols
            )

    row_index = lax.broadcasted_iota(jnp.int32, (dl, cols), 0)

    def contract(chunk, owner):
        for part in range(sectors):
            live = row_index < rows_ref[sec * sectors + part]

            @pl.loop(0, local_terms, unroll=2)
            def _(term):
                whole_term = owner * local_terms + term
                states = ph[part, pl.ds(whole_term * q_chunk, q_chunk)]
                result = lax.dot_general(
                    states.reshape(q_chunk * dl, 2 * cols),
                    rbuf[owner, term, part],
                    (((1,), (1,)), ((), ())),
                    preferred_element_type=jnp.float32,
                )
                for q in range(q_chunk):
                    piece = jnp.where(live, result[q * dl:(q + 1) * dl], 0.0)
                    rt[chunk, whole_term, part, :, q * cols:(q + 1) * cols] = piece.astype(
                        jnp.bfloat16
                    )

    tile = 256

    def partial(chunk, target):
        lefts, places = [], []
        for term in range(terms):
            src = order[term // local_terms, term % local_terms, target] - sec * sectors
            inside = jnp.logical_and(src >= 0, src < sectors)
            place = jnp.clip(src, 0, sectors - 1)
            gate = jnp.where(inside, 1.0, 0.0)
            block = lbuf[term // local_terms, term % local_terms, place]
            lefts.append((block.astype(jnp.float32) * gate).astype(jnp.bfloat16))
            places.append(place)
        lhs = jnp.concatenate(lefts, axis=1)
        for n in range(0, width, tile):
            rhs = jnp.concatenate(
                [rt[chunk, term, places[term], :, n:n + tile] for term in range(terms)], axis=0
            )
            acc[:, n:n + tile] = jnp.dot(lhs, rhs, preferred_element_type=jnp.float32)

    def hop(chunk, owner, part, landing, sems, to):
        return pltpu.make_async_remote_copy(
            src_ref=sendbuf.at[chunk, owner, part], dst_ref=landing.at[chunk, owner, part],
            send_sem=send_sems.at[chunk, owner, part], recv_sem=sems.at[chunk, owner, part],
            device_id={"sec": to}, device_id_type=MESH,
        )

    def pass_on(chunk, owner, part, inner, landing, sems, to):
        partial(chunk, owner * sectors + part)

        @pl.when(inner)
        def _():
            hop(chunk, owner, part, landing, sems, to).wait_recv()
            acc[...] += landing[chunk, owner, part].astype(jnp.float32)

        sendbuf[chunk, owner, part] = acc[...].astype(jnp.bfloat16)
        hop(chunk, owner, part, landing, sems, to).start()

    up = lax.rem(sec + 1, sec_count)
    down = lax.rem(sec + sec_count - 1, sec_count)

    for chunk in range(chunks):
        for part in range(sectors):
            if chunk == 0:
                wave_copies[part].wait()
            transform(chunk, part)
        if chunk == 0:
            own_right.wait()
        contract(chunk, mpo)
        if chunk == 0:
            @pl.when(rep == 0)
            def _():
                for copy in env_copies:
                    copy.wait_send()
                signal(turn, {"rep": 1})

            @pl.when(rep == 1)
            def _():
                pl.semaphore_wait(turn, 1)
                for copy in env_copies:
                    copy.start()

        for step in range(1, mpo_count):
            if chunk == 0:
                right_copies[step - 1].wait_recv()
            contract(chunk, lax.rem(mpo + mpo_count - step, mpo_count))
        if chunk == 0:
            own_left.wait()
            to_scalars.wait()
            for copy in left_copies:
                copy.wait_recv()

        @pl.loop(0, sec_count - 1)
        def _(step):
            above = sec + sec_count - 1 - step
            below = step - (sec_count - 1) + sec

            @pl.when(above < sec_count)
            def _():
                @pl.loop(0, sectors)
                def _(part):
                    pass_on(chunk, above, part, sec > 0, from_left, fl_sems, up)

            @pl.when(below >= 0)
            def _():
                @pl.loop(0, sectors)
                def _(part):
                    pass_on(chunk, below, part, sec < sec_count - 1, from_right, fr_sems, down)

    for chunk in range(chunks):
        for part in range(sectors):
            partial(chunk, sec * sectors + part)

            @pl.when(sec > 0)
            def _():
                hop(chunk, sec, part, from_left, fl_sems, up).wait_recv()
                acc[...] += from_left[chunk, sec, part].astype(jnp.float32)

            @pl.when(sec < sec_count - 1)
            def _():
                hop(chunk, sec, part, from_right, fr_sems, down).wait_recv()
                acc[...] += from_right[chunk, sec, part].astype(jnp.float32)

            live = row_index < rows_ref[sec * sectors + part]
            for q in range(q_chunk):
                piece = acc[:, q * cols:(q + 1) * cols]
                out_ref[part, :, chunk * q_chunk + q, :] = jnp.where(live, piece, 0.0)

    @pl.loop(0, sec_count)
    def _(owner):
        @pl.when(owner != sec)
        def _():
            for chunk in range(chunks):
                for part in range(sectors):
                    hop(chunk, owner, part, from_left, fl_sems, up).wait_send()

    @pl.when(rep == 1)
    def _():
        for copy in env_copies:
            copy.wait_send()


def per_device(sec_count, mpo_count, wave, left_env, right_env, phys_op, source, sector_rows):
    sectors, dl, phys_all, cols = wave.shape
    local_terms = phys_op.shape[0]
    terms = local_terms * mpo_count
    q_here = phys_all // mpo_count
    vmem = pl.BlockSpec(memory_space=pltpu.VMEM)
    smem = pl.BlockSpec(memory_space=pltpu.SMEM)
    chunks = 2 if q_here % 2 == 0 else 1
    q_chunk = q_here // chunks
    width = q_chunk * cols
    bf16 = jnp.bfloat16
    out = pl.pallas_call(
        functools.partial(kernel, sec_count, mpo_count, q_here),
        out_shape=jax.ShapeDtypeStruct((sectors, dl, q_here, cols), jnp.float32),
        in_specs=[vmem, smem, vmem, vmem, vmem, vmem],
        out_specs=vmem,
        scratch_shapes=[
            pltpu.VMEM((mpo_count,) + source.shape, jnp.int32),
            pltpu.SMEM((mpo_count,) + source.shape, jnp.int32),
            pltpu.VMEM((mpo_count,) + phys_op.shape, bf16),
            pltpu.VMEM((terms * q_here * GROUP, terms * phys_all), bf16),
            pltpu.VMEM((chunks, terms * q_chunk * GROUP, GROUP * phys_all), bf16),
            pltpu.VMEM((2, sectors, dl * phys_all, cols), bf16),
            pltpu.VMEM((mpo_count,) + left_env.shape, bf16),
            pltpu.VMEM((mpo_count,) + right_env.shape, bf16),
            pltpu.VMEM((sectors, terms * q_chunk, dl, 2 * cols), bf16),
            pltpu.VMEM((chunks, terms, sectors, dl, width), bf16),
            pltpu.VMEM((dl, width), jnp.float32),
            pltpu.VMEM((chunks, sec_count, sectors, dl, width), bf16),
            pltpu.VMEM((chunks, sec_count, sectors, dl, width), bf16),
            pltpu.VMEM((chunks, sec_count, sectors, dl, width), bf16),
            pltpu.SemaphoreType.DMA((2, sectors)),
            pltpu.SemaphoreType.DMA((2, 2, mpo_count)),
            pltpu.SemaphoreType.DMA((2, mpo_count)),
            pltpu.SemaphoreType.DMA((2, mpo_count)),
            pltpu.SemaphoreType.DMA((chunks, sec_count, sectors)),
            pltpu.SemaphoreType.DMA((chunks, sec_count, sectors)),
            pltpu.SemaphoreType.DMA((chunks, sec_count, sectors)),
            pltpu.SemaphoreType.DMA((4,)),
            pltpu.SemaphoreType.REGULAR,
        ],
        compiler_params=pltpu.CompilerParams(
            collective_id=0, has_side_effects=True, vmem_limit_bytes=56 * 1024 * 1024
        ),
        cost_estimate=pl.CostEstimate(
            flops=6 * 10**9, bytes_accessed=8 * 2**20, transcendentals=0
        ),
    )(
        source, sector_rows, wave.reshape(sectors, dl * phys_all, cols),
        left_env, right_env, phys_op,
    )
    return out


def solution(mesh):
    placed = (
        P(("groups", "sec"), None, None, "rep"),
        P(("groups", "mpo"), "sec", None, None),
        P(("groups", "mpo"), "sec", "rep", None),
        P(("groups", "mpo"), None, None),
        P(("groups", "mpo"), None),
        P("groups"),
    )
    return jax.shard_map(
        functools.partial(per_device, mesh.shape["sec"], mesh.shape["mpo"]),
        mesh=mesh,
        in_specs=placed,
        out_specs=P(("groups", "sec"), None, "mpo", "rep"),
        check_vma=False,
    )
```

time: 60.3 us -> 58.5 us (0.970)
  Pallas kernels: 57.8 us -> 56.1 us
    pallas_call x1, Pallas kernels: 57.8 us -> 56.1 us  [per_device(): pl.pallas_call(functools.partial(kernel, sec_count, mpo_count, q_here), o...]
where the time goes in v3:
time: 58.5 us; the launch traced here: 58.3 us
  Pallas kernels  56.1 us (96%)
  local copies, waits for them, and re-layouts  2.26 us (4%)
    pallas_call x1, Pallas kernels, per_device(): pl.pallas_call(functools.partial(kernel, sec_count, mpo_count, q_here), o...  56.1 us
    unnamed x1, local copies, waits for them, and re-layouts  2.26 us

profile of v3, /device:TPU:1, one launch (start us, length us, event | category | flops | bytes accessed | tf_op | source)
XLA Modules:
  0.0 58.3 jit_solution(3682236281895820141)
XLA Ops:
  0.0 56.1 %shard_map.64 = f32[2,128,8,128]{3,2,1,0:T(8,128)} custom-call(s32[4,8]{1,0:T(4,128)} %source_ref.1, s32[8]{0:T(128)} %rows_ref.1, bf16[2,2048,128]{2,1,0:T(8,128)(2,1)} %bitcast.1, bf16[4,2,128,128]{3,2,1,0:T(8,128)(2,1)} %left_ref.1, bf16[4,2,128,256]{3,2,1,0:T(8,128)(2,1)} %right_ref.1, bf16[4,16,16]{2,1,0:T(8,128)(2,1)} %phys_ref.1), custom_call_target="tpu_custom_call" | custom-call | flops 6000000000 | bytes 8388608 | tf_op jit(solution)/shard_map/pallas_call | solution.py:292
  56.1 2.3 %copy.8 = f32[2,128,8,128]{3,2,1,0:T(8,128)} copy(f32[2,128,8,128]{3,2,1,0:T(8,128)} %shard_map.64) | data formatting | bytes 2097152

commit v4 on v3

--- a/solution.py
+++ b/solution.py
@@ -157,7 +157,7 @@
                         jnp.bfloat16
                     )
 
-    tile = 256
+    tile = min(256, width)
 
     def partial(chunk, target):
         lefts, places = [], []
@@ -197,15 +197,15 @@
     up = lax.rem(sec + 1, sec_count)
     down = lax.rem(sec + sec_count - 1, sec_count)
 
-    for chunk in range(chunks):
+    def one_chunk(chunk, first):
         for part in range(sectors):
-            if chunk == 0:
+            if first:
                 wave_copies[part].wait()
             transform(chunk, part)
-        if chunk == 0:
+        if first:
             own_right.wait()
         contract(chunk, mpo)
-        if chunk == 0:
+        if first:
             @pl.when(rep == 0)
             def _():
                 for copy in env_copies:
@@ -219,10 +219,10 @@
                     copy.start()
 
         for step in range(1, mpo_count):
-            if chunk == 0:
+            if first:
                 right_copies[step - 1].wait_recv()
             contract(chunk, lax.rem(mpo + mpo_count - step, mpo_count))
-        if chunk == 0:
+        if first:
             own_left.wait()
             to_scalars.wait()
             for copy in left_copies:
@@ -244,6 +244,12 @@
                 @pl.loop(0, sectors)
                 def _(part):
                     pass_on(chunk, below, part, sec < sec_count - 1, from_right, fr_sems, down)
+
+    one_chunk(0, True)
+
+    @pl.loop(1, chunks)
+    def _(chunk):
+        one_chunk(chunk, False)
 
     for chunk in range(chunks):
         for part in range(sectors):
@@ -285,7 +291,7 @@
     q_here = phys_all // mpo_count
     vmem = pl.BlockSpec(memory_space=pltpu.VMEM)
     smem = pl.BlockSpec(memory_space=pltpu.SMEM)
-    chunks = 2 if q_here % 2 == 0 else 1
+    chunks = 4 if q_here % 4 == 0 else 1
     q_chunk = q_here // chunks
     width = q_chunk * cols
     bf16 = jnp.bfloat16

time: 58.5 us -> 65.3 us (1.12)
  Pallas kernels: 56.1 us -> 62.3 us
    pallas_call x1, Pallas kernels: 56.1 us -> 62.3 us  [per_device(): pl.pallas_call(functools.partial(kernel, sec_count, mpo_count, q_here), o...]
where the time goes in v4:
time: 65.3 us; the launch traced here: 64.6 us
  Pallas kernels  62.3 us (95%)
  local copies, waits for them, and re-layouts  2.26 us (3%)
    pallas_call x1, Pallas kernels, per_device(): pl.pallas_call(functools.partial(kernel, sec_count, mpo_count, q_here), o...  62.3 us
    unnamed x1, local copies, waits for them, and re-layouts  2.26 us

profile of v4, /device:TPU:1, one launch (start us, length us, event | category | flops | bytes accessed | tf_op | source)
XLA Modules:
  0.0 64.6 jit_solution(215447956855419934)
XLA Ops:
  0.0 62.3 %shard_map.64 = f32[2,128,8,128]{3,2,1,0:T(8,128)} custom-call(s32[4,8]{1,0:T(4,128)} %source_ref.1, s32[8]{0:T(128)} %rows_ref.1, bf16[2,2048,128]{2,1,0:T(8,128)(2,1)} %bitcast.1, bf16[4,2,128,128]{3,2,1,0:T(8,128)(2,1)} %left_ref.1, bf16[4,2,128,256]{3,2,1,0:T(8,128)(2,1)} %right_ref.1, bf16[4,16,16]{2,1,0:T(8,128)(2,1)} %phys_ref.1), custom_call_target="tpu_custom_call" | custom-call | flops 6000000000 | bytes 8388608 | tf_op jit(solution)/shard_map/pallas_call | solution.py:298
  62.3 2.3 %copy.8 = f32[2,128,8,128]{3,2,1,0:T(8,128)} copy(f32[2,128,8,128]{3,2,1,0:T(8,128)} %shard_map.64) | data formatting | bytes 2097152

commit v5 on v3

--- a/solution.py
+++ b/solution.py
@@ -197,7 +197,7 @@
     up = lax.rem(sec + 1, sec_count)
     down = lax.rem(sec + sec_count - 1, sec_count)
 
-    for chunk in range(chunks):
+    def build(chunk):
         for part in range(sectors):
             if chunk == 0:
                 wave_copies[part].wait()
@@ -228,6 +228,7 @@
             for copy in left_copies:
                 copy.wait_recv()
 
+    def send(chunk):
         @pl.loop(0, sec_count - 1)
         def _(step):
             above = sec + sec_count - 1 - step
@@ -244,6 +245,20 @@
                 @pl.loop(0, sectors)
                 def _(part):
                     pass_on(chunk, below, part, sec < sec_count - 1, from_right, fr_sems, down)
+
+    at_end = jnp.logical_or(sec == 0, sec == sec_count - 1)
+    build(0)
+    for chunk in range(chunks):
+        if chunk + 1 < chunks:
+            @pl.when(jnp.logical_not(at_end))
+            def _():
+                build(chunk + 1)
+
+        send(chunk)
+        if chunk + 1 < chunks:
+            @pl.when(at_end)
+            def _():
+                build(chunk + 1)
 
     for chunk in range(chunks):
         for part in range(sectors):

time: 58.5 us -> 58.5 us (level)
  no operation moved by 1% of the time
where the time goes in v5:
time: 58.5 us; the launch traced here: 58.3 us
  Pallas kernels  56.1 us (96%)
  local copies, waits for them, and re-layouts  2.26 us (4%)
    pallas_call x1, Pallas kernels, per_device(): pl.pallas_call(functools.partial(kernel, sec_count, mpo_count, q_here), o...  56.1 us
    unnamed x1, local copies, waits for them, and re-layouts  2.26 us

profile of v5, /device:TPU:1, one launch (start us, length us, event | category | flops | bytes accessed | tf_op | source)
XLA Modules:
  0.0 58.3 jit_solution(11502969001142532950)
XLA Ops:
  0.0 56.1 %shard_map.64 = f32[2,128,8,128]{3,2,1,0:T(8,128)} custom-call(s32[4,8]{1,0:T(4,128)} %source_ref.1, s32[8]{0:T(128)} %rows_ref.1, bf16[2,2048,128]{2,1,0:T(8,128)(2,1)} %bitcast.1, bf16[4,2,128,128]{3,2,1,0:T(8,128)(2,1)} %left_ref.1, bf16[4,2,128,256]{3,2,1,0:T(8,128)(2,1)} %right_ref.1, bf16[4,16,16]{2,1,0:T(8,128)(2,1)} %phys_ref.1), custom_call_target="tpu_custom_call" | custom-call | flops 6000000000 | bytes 8388608 | tf_op jit(solution)/shard_map/pallas_call | solution.py:307
  56.1 2.3 %copy.8 = f32[2,128,8,128]{3,2,1,0:T(8,128)} copy(f32[2,128,8,128]{3,2,1,0:T(8,128)} %shard_map.64) | data formatting | bytes 2097152
